TPU v7x, 256 devices: a whole 4x4x8 slice. The times are simulated.
256 devices in a mesh: seq: 32 (over x, z), fsdp: 8 (over y, core).
Axes of the slice: x: 4, y: 4, z: 8, core: 2. Of those that a mesh axis runs over, the one named last changes fastest.
Arguments:
- frames: bfloat16 [8, 4096, 1536], P('fsdp', 'seq'), may hold values from -6 to 6
- lengths: int32 [8, 4], P('fsdp'), may hold values from 1 to 2048, 4096 in all within a row
- offsets: int32 [8, 33], P('fsdp'), may hold values from 0 to 4096, as said below
- w_in: bfloat16 [1536, 3072], P('fsdp'), may hold values from -0.15625 to 0.15625
- kernel: float32 [31, 1536], replicated, may hold values from -1 to 1
- cotangent: bfloat16 [8, 8192, 1536], P('fsdp', 'seq'), may hold values from -6 to 6
Outputs:
- owner_output: bfloat16 [8, 8192, 1536], P('fsdp', 'seq')
- frame_grad: bfloat16 [8, 4096, 1536], P('fsdp', 'seq')
- w_grad: float32 [1536, 3072], P(('seq', 'fsdp'))
Inputs may be any that keep to these rules, and one draw needn't show every extreme that they name: Row g: device i of seq owns the frames offsets[g, i] to offsets[g, i + 1] - 1; offsets[g, 0] = 0 and offsets[g, 32] = 4096; each device owns 128 // 4 to 256 frames, beginning within 64 of i * 128; in every group one device owns exactly 256. `lengths`: each row sums to 4096; its largest entry is exactly 2048.
All inputs are finite; a program needn't handle non-finite values.
Results may differ from a plain program's by a relative error of at most 0.025.
Values may be sent and summed in bfloat16 or wider, within the bound.
No kernel may reach another device: no remote copies, remote signals or barrier semaphores. Data moves between devices by JAX's collectives and lax.ppermute only.
A program may use at most 128 MiB of HBM per device.

v0:
```python
import math
import jax
import jax.numpy as jnp
from jax import lax
from jax.sharding import PartitionSpec as P

epsilon = 1e-05


def passed_along(value, axis, steps):
    count = lax.axis_size(axis)
    initial, last = (max(0, -steps), min(count, count - steps))
    return lax.ppermute(value, axis, [(source, source + steps) for source in range(initial, last)])


def normalize_rows(values):
    values = values.astype(jnp.float32)
    center = jnp.mean(values, axis=-1, keepdims=True)
    shifted = values - center
    scale_inv = lax.rsqrt(jnp.mean(shifted * shifted, axis=-1, keepdims=True) + epsilon)
    return (shifted * scale_inv, scale_inv)


def norm_backward(upstream, normed, scale_inv):
    first_mean = jnp.mean(upstream, axis=-1, keepdims=True)
    second_mean = jnp.mean(upstream * normed, axis=-1, keepdims=True)
    return scale_inv * (upstream - first_mean - normed * second_mean)


def depthwise(window, kernel, labels, row_count):
    tap_count = kernel.shape[0]
    half_width = tap_count // 2
    centre = labels[half_width : half_width + row_count]
    result = jnp.zeros((row_count, kernel.shape[1]), jnp.float32)
    for tap_index in range(tap_count):
        same_utt = (labels[tap_index : tap_index + row_count] == centre).astype(jnp.float32)
        result = (
            result
            + kernel[tap_index]
            * window[tap_index : tap_index + row_count].astype(jnp.float32)
            * same_utt[:, None]
        )
    return result


def depthwise_back(window, kernel, labels, row_count):
    tap_count = kernel.shape[0]
    half_width = tap_count // 2
    centre = labels[half_width : half_width + row_count]
    result = jnp.zeros((row_count, kernel.shape[1]), jnp.float32)
    for tap_index in range(tap_count):
        tap_row = 2 * half_width - tap_index
        same_utt = (labels[tap_row : tap_row + row_count] == centre).astype(jnp.float32)
        result = (
            result + kernel[tap_index] * window[tap_row : tap_row + row_count] * same_utt[:, None]
        )
    return result


def finish(d_glu, values, gates, hidden, normed, scale_inv, backward_product):
    d_mixed = jnp.concatenate(
        [d_glu * gates, d_glu * values * gates * (1.0 - gates)], axis=1
    ).astype(jnp.bfloat16)
    d_hidden = backward_product(d_mixed)
    d_rows = norm_backward(d_hidden, normed, scale_inv).astype(jnp.bfloat16)
    partial_sum = lax.dot_general(
        hidden, d_mixed, (((0,), (0,)), ((), ())), preferred_element_type=jnp.float32
    )
    return (d_rows, partial_sum)


def on_device(frames, lengths, offsets, w_in, kernel, cotangent):
    rows_in = frames[0]
    per_device = rows_in.shape[0]
    model_width = rows_in.shape[1]
    capacity = 2 * per_device
    seq_count = lax.axis_size("seq")
    group_count = lax.axis_size("fsdp")
    device = lax.axis_index("seq")
    frame_total = seq_count * per_device
    half_width = kernel.shape[0] // 2
    bounds_row = offsets[0]
    start_row = bounds_row[device]
    owned_load = bounds_row[device + 1] - start_row
    base_row = (device - 1) * per_device
    utt_bounds = jnp.cumsum(lengths[0])[:-1]
    slot_index = jnp.arange(capacity, dtype=jnp.int32)
    owned = (slot_index < owned_load)[:, None]
    bf_zero = jnp.zeros((), jnp.bfloat16)
    cot_rows = jnp.where(owned, cotangent[0], bf_zero)

    def backward_product(d_mixed):
        return lax.dot_general(
            d_mixed,
            lax.all_gather(w_in, "fsdp", axis=0, tiled=True),
            (((1,), (1,)), ((), ())),
            preferred_element_type=jnp.float32,
        )

    from_prev = passed_along(rows_in, "seq", 1)
    from_next = passed_along(rows_in, "seq", -1)
    gathered = jnp.concatenate([from_prev, rows_in, from_next, jnp.zeros_like(rows_in)], axis=0)
    window_rows = capacity + 2 * half_width
    rows_window = lax.dynamic_slice_in_dim(
        gathered, start_row - half_width - base_row, window_rows, 0
    )
    positions = start_row - half_width + jnp.arange(window_rows, dtype=jnp.int32)
    labels = jnp.sum((positions[:, None] >= utt_bounds[None, :]).astype(jnp.int32), axis=1)
    inside = (positions >= 0) & (positions < frame_total)
    labels = jnp.where(inside, labels, -1)
    normed, scale_inv = normalize_rows(rows_window)
    hidden = normed.astype(jnp.bfloat16)
    projected = jnp.dot(
        hidden, lax.all_gather(w_in, "fsdp", axis=0, tiled=True), preferred_element_type=jnp.float32
    )
    values = projected[:, :model_width]
    gates = jax.nn.sigmoid(projected[:, model_width:])
    glu_out = (values * gates).astype(jnp.bfloat16)
    conv = depthwise(glu_out, kernel, labels, capacity)
    conv_normed, conv_inv = normalize_rows(conv)
    gate_out = jax.nn.sigmoid(conv_normed)
    output = conv_normed * gate_out
    owner_output = jnp.where(owned, output.astype(jnp.bfloat16), bf_zero)
    upstream = cot_rows.astype(jnp.float32)
    d_normed = upstream * (gate_out + output * (1.0 - gate_out))
    d_conv = jnp.where(owned, norm_backward(d_normed, conv_normed, conv_inv), 0.0)
    tail_rows = lax.dynamic_slice_in_dim(d_conv, owned_load - half_width, half_width, 0)
    head_rows = d_conv[:half_width]
    left_part = passed_along(tail_rows.astype(jnp.bfloat16), "seq", 1).astype(tail_rows.dtype)
    right_part = passed_along(head_rows.astype(jnp.bfloat16), "seq", -1).astype(head_rows.dtype)
    edge_zeros = jnp.zeros((half_width, model_width), jnp.float32)
    d_window = jnp.concatenate([left_part, d_conv, edge_zeros], axis=0)
    right_placed = lax.dynamic_update_slice_in_dim(
        jnp.zeros((window_rows, model_width), jnp.float32), right_part, half_width + owned_load, 0
    )
    d_window = d_window + right_placed
    d_glu = jnp.where(owned, depthwise_back(d_window, kernel, labels, capacity), 0.0)
    inner_end = half_width + capacity
    d_rows, partial_sum = finish(
        d_glu,
        values[half_width:inner_end],
        gates[half_width:inner_end],
        hidden[half_width:inner_end],
        normed[half_width:inner_end],
        scale_inv[half_width:inner_end],
        backward_product,
    )
    placed = lax.dynamic_update_slice_in_dim(
        jnp.zeros((4 * per_device, model_width), jnp.bfloat16), d_rows, start_row - base_row, 0
    )
    back_prev = passed_along(placed[:per_device], "seq", -1)
    back_next = passed_along(placed[2 * per_device : 3 * per_device], "seq", 1)
    frame_grad = (
        placed[per_device : 2 * per_device].astype(jnp.float32)
        + back_prev.astype(jnp.float32)
        + back_next.astype(jnp.float32)
    ).astype(jnp.bfloat16)
    rounded = lax.optimization_barrier(partial_sum.astype(jnp.bfloat16)).astype(jnp.float32)
    seq_summed = lax.psum_scatter(
        rounded.astype(jnp.bfloat16), "seq", scatter_dimension=0, tiled=True
    )
    summed = lax.psum_scatter(seq_summed, "fsdp", scatter_dimension=0, tiled=True).astype(
        jnp.float32
    )
    w_grad = summed * (1.0 / math.sqrt(group_count * frame_total))
    return (owner_output[None], frame_grad[None], w_grad)


def solution(mesh):
    return jax.shard_map(
        on_device,
        mesh=mesh,
        in_specs=(
            P("fsdp", "seq", None),
            P("fsdp", None),
            P("fsdp", None),
            P("fsdp", None),
            P(),
            P("fsdp", "seq", None),
        ),
        out_specs=(P("fsdp", "seq", None), P("fsdp", "seq", None), P(("seq", "fsdp"), None)),
        check_vma=False,
    )
```

profile of v0, /device:TPU:8, one launch (start us, length us, event | category | flops | bytes accessed | tf_op | source)
XLA Modules:
  0.0 391.4 jit_solution(15712493318630391508)
XLA Ops:
  7.2 0.0 all-gather.2.cloned.1.call-start
  7.2 0.7 all-gather.2.cloned.1.call-update
  7.9 0.0 reduce-scatter.4.cloned.1.call-start
  8.0 3.8 collective-permute-start
  11.8 1.3 collective-permute-start.1
  13.1 1.4 constant_dynamic-slice_fusion.1
  15.2 0.8 reduce-window.4
  17.4 0.1 pad_dynamic-slice_fusion.3
  17.5 0.1 convert_reduce_fusion.1
  17.6 1.6 slice_reduce_fusion.29
  19.3 0.0 copy-start.26
  19.3 0.0 copy-start.27
  19.3 0.1 compare_convert_fusion.26
  19.4 0.1 compare_convert_fusion.29
  19.6 0.6 compare_convert_fusion.28
  20.3 0.5 iota_compare_fusion
  20.8 1.8 slice_reduce_fusion.30
  22.6 0.0 copy-start.11
  22.7 0.7 compare_convert_fusion.27
  23.4 1.3 collective-permute-done.1
  24.7 0.9 convert_reduce_fusion
  25.6 0.4 fusion.3
  26.0 1.5 fusion.1
  27.6 41.1 %all-gather.2.cloned.1.call-done = bf16[1536,3072]{1,0:T(8,128)(2,1)} async-done(((bf16[192,3072]{1,0:T(8,128)(2,1)}), bf16[1536,3072]{1,0:T(8,128)(2,1)}) %all-gather.2.cloned.1.call-update) | async-done | bytes 9437200 | tf_op jit(solution)/shard_map/all_gather | solution.py:114
  68.7 5.4 %fusion.90 = f32[286,3072]{1,0:T(8,128)S(1)} fusion(bf16[286,1536]{1,0:T(8,128)(2,1)S(1)} %get-tuple-element.52, bf16[1536,3072]{1,0:T(8,128)(2,1)} %all-gather.2.cloned.1.call-done), kind=kOutput, calls=%fused_computation.223 | convolution fusion | flops 2699034624 | bytes 13830144 | tf_op jit(solution)/shard_map/dot_general | solution.py:113
  74.2 2.1 fusion.6
  76.2 0.3 copy-done.1
  76.9 13.3 %fusion.86 = (f32[256]{0:T(256)S(1)}, f32[256,1536]{1,0:T(8,128)S(1)}) fusion(f32[256]{0:T(256)S(1)} %get-tuple-element.82, bf16[286,1536]{1,0:T(8,128)(2,1)S(1)} %get-tuple-element.46, f32[1536]{0:T(1024)S(1)} %get-tuple-element.36, f32[256]{0:T(256)S(1)} %get-tuple-element.54, f32[1536]{0:T(1024)S(1)} %get-tuple-element.37, f32[256]{0:T(256)S(1)} %get-tuple-element.55, ...), kind=kLoop, calls=%fused_computation.220 | loop fusion | flops 48365312 | bytes 26174464 | tf_op jit(solution)/shard_map/reduce_sum | solution.py:18
  90.2 0.0 copy-start.7
  90.2 0.3 multiply_reduce_fusion.2
  90.5 0.8 copy-done.7
  91.3 1.7 fusion.84
  93.0 1.1 multiply_select_fusion
  94.2 1.1 copy-done.2
  95.3 3.5 collective-permute-start.2
  98.8 0.7 pad.4.clone
  99.5 1.5 collective-permute-start.3
  101.0 1.6 maximum_maximum_fusion
  102.6 2.9 collective-permute-done.3
  105.5 0.8 add.319
  106.2 10.6 %multiply_convert_fusion.1 = (bf16[256,1536]{1,0:T(8,128)(2,1)S(1)}, f32[256,1536]{1,0:T(8,128)S(1)}) fusion(f32[286,1536]{1,0:T(8,128)} %get-tuple-element.45, f32[256]{0:T(256)} %copy-done.37, f32[286,1536]{1,0:T(8,128)S(1)} %add.319, f32[1536]{0:T(1024)} %copy-done.26, f32[256]{0:T(256)} %copy-done.46, f32[1536]{0:T(1024)} %copy-done.27, ...), kind=kLoop, calls=%fused_computation.115 | loop fusion | flops 36962304 | bytes 52912384 | tf_op jit(solution)/shard_map/convert
  116.9 2.3 fusion.10
  119.2 0.9 copy-done.8
  120.0 5.2 %convolution_convert_fusion = bf16[1536,3072]{1,0:T(8,128)(2,1)} fusion(bf16[256,1536]{1,0:T(8,128)(2,1)S(1)} %fusion.10, bf16[256,1536]{1,0:T(8,128)(2,1)S(1)} %get-tuple-element.38, bf16[286,1536]{1,0:T(8,128)(2,1)S(1)} %copy-done.6), kind=kOutput, calls=%fused_computation | convolution fusion | flops 2423783424 | bytes 11796480 | tf_op jit(solution)/shard_map/dot_general | solution.py:66
  125.3 0.0 reduce-scatter.4.cloned.1.call-update
  126.1 0.6 dynamic-slice.8
  127.4 0.1 slice.572
  127.5 2.1 select_bitcast_fusion
  129.5 5.9 %fusion.83 = (f32[256]{0:T(256)S(1)}, f32[256]{0:T(256)S(1)}, f32[256,1536]{1,0:T(8,128)S(1)}) fusion(f32[286,1536]{1,0:T(8,128)S(1)} %copy-done.3, bf16[1536,3072]{1,0:T(8,128)(2,1)} %all-gather.2.cloned.1.call-done, bf16[256,1536]{1,0:T(8,128)(2,1)} %copy-done.8, bf16[256,1536]{1,0:T(8,128)(2,1)} %copy-done.9), kind=kOutput, calls=%fused_computation.218 | convolution fusion | flops 2420243968 | bytes 14157824 | tf_op jit(solution)/shard_map/dot_general | solution.py:93
  135.5 1.3 multiply_convert_fusion
  136.7 0.1 broadcast_in_dim.45
  136.8 1.0 copy-done.4
  137.9 4.0 %dynamic_update_slice.7 = bf16[512,1536]{1,0:T(8,128)(2,1)S(1)} dynamic-update-slice(bf16[512,1536]{1,0:T(8,128)(2,1)S(1)} %broadcast_in_dim.45, bf16[256,1536]{1,0:T(8,128)(2,1)S(1)} %copy-done.4, s32[]{:T(128)S(6)} %select_n.46, s32[]{:T(128)} %constant.22.clone.1) | dynamic-update-slice | bytes 1572868 | tf_op jit(solution)/shard_map/dynamic_update_slice | solution.py:148
  141.9 0.1 fusion.88
  141.9 1.3 collective-permute-start.4
  143.2 4.6 %collective-permute-start.5 = (bf16[128,1536]{1,0:T(8,128)(2,1)S(1)}, bf16[128,1536]{1,0:T(8,128)(2,1)S(1)}, u32[]{:S(2)}, u32[]{:S(2)}) collective-permute-start(bf16[128,1536]{1,0:T(8,128)(2,1)S(1)} %get-tuple-element.48), channel_id=1, source_target_pairs={{0,8},{8,16},{16,24},{24,32},{32,40},{40,48},{48,56},{56,64},{64,7... | collective-permute-start | bytes 1179656 | tf_op jit(solution)/shard_map/ppermute | solution.py:13
  147.8 212.4 %reduce-scatter.4.cloned.1.call-done = bf16[48,3072]{1,0:T(8,128)(2,1)} async-done(((bf16[1536,3072]{1,0:T(8,128)(2,1)}), bf16[48,3072]{1,0:T(8,128)(2,1)}) %reduce-scatter.4.cloned.1.call-update) | async-done | bytes 294928 | tf_op jit(solution)/shard_map/reduce_scatter | solution.py:159
  360.2 14.8 %fusion = bf16[8,3072]{1,0:T(8,128)(2,1)S(1)} fusion(bf16[48,3072]{1,0:T(8,128)(2,1)} %reduce-scatter.4.cloned.1.call-done), kind=kCustom, calls=%all-reduce-scatter | all-reduce-scatter fusion | flops 196609 | bytes 345088
  375.0 1.9 collective-permute-start.6
  376.9 2.1 collective-permute-start.7
  379.0 0.9 fusion.79
  379.9 3.6 collective-permute-done.7
  383.6 0.3 concatenate.16
  383.9 0.7 convert_multiply_fusion
  (120 shorter events, 0.3 us)
Async XLA Ops:
  7.2 17.5 %copy-start.10 = (bf16[1,128,1536]{2,1,0:T(8,128)(2,1)S(1)}, bf16[1,128,1536]{2,1,0:T(8,128)(2,1)}, u32[]{:S(2)}) copy-start(bf16[1,128,1536]{2,1,0:T(8,128)(2,1)} %param.6) | copy-start | bytes 1179652
  7.2 61.5 %all-gather.2.cloned.1.call-start = ((), (), s32[]{:S(2)}) async-start(), calls=%async_computation.1 | async-start | bytes 10616832 | tf_op jit(solution)/shard_map/all_gather | solution.py:114
  7.9 352.3 %reduce-scatter.4.cloned.1.call-start = ((), (), s32[]{:S(2)}) async-start(), calls=%async_computation.2 | async-start | bytes 9732096 | tf_op jit(solution)/shard_map/reduce_scatter | solution.py:159
  8.0 15.4 %collective-permute-start = (bf16[128,1536]{1,0:T(8,128)(2,1)}, bf16[128,1536]{1,0:T(8,128)(2,1)S(1)}, u32[]{:S(2)}, u32[]{:S(2)}) collective-permute-start(bf16[128,1536]{1,0:T(8,128)(2,1)} %bitcast.21), channel_id=1, source_target_pairs={{0,8},{8,16},{16,24},{24,32},{32,40},{40,48},{48,56},{56,64},{64,7... | collective-permute-start | bytes 1179656 | tf_op jit(solution)/shard_map/ppermute | solution.py:13
  11.8 12.8 %collective-permute-start.1 = (bf16[128,1536]{1,0:T(8,128)(2,1)}, bf16[128,1536]{1,0:T(8,128)(2,1)S(1)}, u32[]{:S(2)}, u32[]{:S(2)}) collective-permute-start(bf16[128,1536]{1,0:T(8,128)(2,1)} %bitcast.22), channel_id=1, source_target_pairs={{8,0},{16,8},{24,16},{32,24},{40,32},{48,40},{56,48},{64,56},{72,6... | collective-permute-start | bytes 1179656 | tf_op jit(solution)/shard_map/ppermute | solution.py:13
  19.2 57.3 %copy-start.16 = (f32[1536]{0:T(1024)}, f32[1536]{0:T(1024)S(1)}, u32[]{:S(2)}) copy-start(f32[1536]{0:T(1024)S(1)} %get-tuple-element.26) | copy-start | bytes 18436
  19.2 57.3 %copy-start.17 = (f32[1536]{0:T(1024)}, f32[1536]{0:T(1024)S(1)}, u32[]{:S(2)}) copy-start(f32[1536]{0:T(1024)S(1)} %get-tuple-element.27) | copy-start | bytes 18436
  19.2 57.3 %copy-start.18 = (f32[1536]{0:T(1024)}, f32[1536]{0:T(1024)S(1)}, u32[]{:S(2)}) copy-start(f32[1536]{0:T(1024)S(1)} %get-tuple-element.28) | copy-start | bytes 18436
  19.2 57.3 %copy-start.19 = (f32[1536]{0:T(1024)}, f32[1536]{0:T(1024)S(1)}, u32[]{:S(2)}) copy-start(f32[1536]{0:T(1024)S(1)} %get-tuple-element.29) | copy-start | bytes 18436
  19.3 57.3 %copy-start.20 = (f32[1536]{0:T(1024)}, f32[1536]{0:T(1024)S(1)}, u32[]{:S(2)}) copy-start(f32[1536]{0:T(1024)S(1)} %get-tuple-element.30) | copy-start | bytes 18436
  19.3 57.3 %copy-start.21 = (f32[1536]{0:T(1024)}, f32[1536]{0:T(1024)S(1)}, u32[]{:S(2)}) copy-start(f32[1536]{0:T(1024)S(1)} %get-tuple-element.31) | copy-start | bytes 18436
  19.3 57.3 %copy-start.22 = (f32[1536]{0:T(1024)}, f32[1536]{0:T(1024)S(1)}, u32[]{:S(2)}) copy-start(f32[1536]{0:T(1024)S(1)} %get-tuple-element.32) | copy-start | bytes 18436
  19.3 57.3 %copy-start.23 = (f32[1536]{0:T(1024)}, f32[1536]{0:T(1024)S(1)}, u32[]{:S(2)}) copy-start(f32[1536]{0:T(1024)S(1)} %get-tuple-element.33) | copy-start | bytes 18436
  19.3 57.3 %copy-start.24 = (f32[1536]{0:T(1024)}, f32[1536]{0:T(1024)S(1)}, u32[]{:S(2)}) copy-start(f32[1536]{0:T(1024)S(1)} %get-tuple-element.34) | copy-start | bytes 18436
  19.3 57.3 %copy-start.25 = (f32[1536]{0:T(1024)}, f32[1536]{0:T(1024)S(1)}, u32[]{:S(2)}) copy-start(f32[1536]{0:T(1024)S(1)} %get-tuple-element.35) | copy-start | bytes 18436
  19.3 57.3 %copy-start.26 = (f32[1536]{0:T(1024)}, f32[1536]{0:T(1024)S(1)}, u32[]{:S(2)}) copy-start(f32[1536]{0:T(1024)S(1)} %get-tuple-element.36) | copy-start | bytes 18436
  19.3 57.3 %copy-start.27 = (f32[1536]{0:T(1024)}, f32[1536]{0:T(1024)S(1)}, u32[]{:S(2)}) copy-start(f32[1536]{0:T(1024)S(1)} %get-tuple-element.37) | copy-start | bytes 18436
  19.4 57.2 %copy-start.34 = (f32[256]{0:T(256)}, f32[256]{0:T(256)S(1)}, u32[]{:S(2)}) copy-start(f32[256]{0:T(256)S(1)} %get-tuple-element.80) | copy-start | bytes 3076
  19.4 57.2 %copy-start.35 = (f32[256]{0:T(256)}, f32[256]{0:T(256)S(1)}, u32[]{:S(2)}) copy-start(f32[256]{0:T(256)S(1)} %get-tuple-element.81) | copy-start | bytes 3076
  19.4 57.2 %copy-start.36 = (f32[256]{0:T(256)}, f32[256]{0:T(256)S(1)}, u32[]{:S(2)}) copy-start(f32[256]{0:T(256)S(1)} %get-tuple-element.82) | copy-start | bytes 3076
  19.5 57.2 %copy-start.37 = (f32[256]{0:T(256)}, f32[256]{0:T(256)S(1)}, u32[]{:S(2)}) copy-start(f32[256]{0:T(256)S(1)} %get-tuple-element.53) | copy-start | bytes 3076
  19.5 57.2 %copy-start.38 = (f32[256]{0:T(256)}, f32[256]{0:T(256)S(1)}, u32[]{:S(2)}) copy-start(f32[256]{0:T(256)S(1)} %get-tuple-element.54) | copy-start | bytes 3076
  19.5 57.2 %copy-start.39 = (f32[256]{0:T(256)}, f32[256]{0:T(256)S(1)}, u32[]{:S(2)}) copy-start(f32[256]{0:T(256)S(1)} %get-tuple-element.55) | copy-start | bytes 3076
  19.5 57.2 %copy-start.40 = (f32[256]{0:T(256)}, f32[256]{0:T(256)S(1)}, u32[]{:S(2)}) copy-start(f32[256]{0:T(256)S(1)} %get-tuple-element.56) | copy-start | bytes 3076
  19.6 57.2 %copy-start.41 = (f32[256]{0:T(256)}, f32[256]{0:T(256)S(1)}, u32[]{:S(2)}) copy-start(f32[256]{0:T(256)S(1)} %get-tuple-element.57) | copy-start | bytes 3076
  19.6 57.2 %copy-start.42 = (f32[256]{0:T(256)}, f32[256]{0:T(256)S(1)}, u32[]{:S(2)}) copy-start(f32[256]{0:T(256)S(1)} %get-tuple-element.58) | copy-start | bytes 3076
  19.6 57.2 %copy-start.43 = (f32[256]{0:T(256)}, f32[256]{0:T(256)S(1)}, u32[]{:S(2)}) copy-start(f32[256]{0:T(256)S(1)} %get-tuple-element.59) | copy-start | bytes 3076
  19.6 57.2 %copy-start.44 = (f32[256]{0:T(256)}, f32[256]{0:T(256)S(1)}, u32[]{:S(2)}) copy-start(f32[256]{0:T(256)S(1)} %get-tuple-element.60) | copy-start | bytes 3076
  19.6 57.2 %copy-start.45 = (f32[256]{0:T(256)}, f32[256]{0:T(256)S(1)}, u32[]{:S(2)}) copy-start(f32[256]{0:T(256)S(1)} %get-tuple-element.61) | copy-start | bytes 3076
  20.2 56.5 %copy-start.46 = (f32[256]{0:T(256)}, f32[256]{0:T(256)S(1)}, u32[]{:S(2)}) copy-start(f32[256]{0:T(256)S(1)} %get-tuple-element.62) | copy-start | bytes 3076
  20.2 56.5 %copy-start.47 = (f32[256]{0:T(256)}, f32[256]{0:T(256)S(1)}, u32[]{:S(2)}) copy-start(f32[256]{0:T(256)S(1)} %get-tuple-element.63) | copy-start | bytes 3076
  20.2 56.5 %copy-start.48 = (f32[256]{0:T(256)}, f32[256]{0:T(256)S(1)}, u32[]{:S(2)}) copy-start(f32[256]{0:T(256)S(1)} %get-tuple-element.64) | copy-start | bytes 3076
  20.2 56.6 %copy-start.49 = (f32[256]{0:T(256)}, f32[256]{0:T(256)S(1)}, u32[]{:S(2)}) copy-start(f32[256]{0:T(256)S(1)} %get-tuple-element.65) | copy-start | bytes 3076
  20.2 56.6 %copy-start.50 = (f32[256]{0:T(256)}, f32[256]{0:T(256)S(1)}, u32[]{:S(2)}) copy-start(f32[256]{0:T(256)S(1)} %get-tuple-element.66) | copy-start | bytes 3076
  20.2 56.6 %copy-start.51 = (f32[256]{0:T(256)}, f32[256]{0:T(256)S(1)}, u32[]{:S(2)}) copy-start(f32[256]{0:T(256)S(1)} %get-tuple-element.67) | copy-start | bytes 3076
  20.3 56.6 %copy-start.52 = (f32[256]{0:T(256)}, f32[256]{0:T(256)S(1)}, u32[]{:S(2)}) copy-start(f32[256]{0:T(256)S(1)} %get-tuple-element.68) | copy-start | bytes 3076
  22.6 54.2 %copy-start.11 = (f32[1536]{0:T(1024)}, f32[1536]{0:T(1024)S(1)}, u32[]{:S(2)}) copy-start(f32[1536]{0:T(1024)S(1)} %get-tuple-element.21) | copy-start | bytes 18436
  22.6 54.2 %copy-start.12 = (f32[1536]{0:T(1024)}, f32[1536]{0:T(1024)S(1)}, u32[]{:S(2)}) copy-start(f32[1536]{0:T(1024)S(1)} %get-tuple-element.22) | copy-start | bytes 18436
  22.6 54.2 %copy-start.13 = (f32[1536]{0:T(1024)}, f32[1536]{0:T(1024)S(1)}, u32[]{:S(2)}) copy-start(f32[1536]{0:T(1024)S(1)} %get-tuple-element.23) | copy-start | bytes 18436
  22.6 54.2 %copy-start.14 = (f32[1536]{0:T(1024)}, f32[1536]{0:T(1024)S(1)}, u32[]{:S(2)}) copy-start(f32[1536]{0:T(1024)S(1)} %get-tuple-element.24) | copy-start | bytes 18436
  22.7 54.2 %copy-start.15 = (f32[1536]{0:T(1024)}, f32[1536]{0:T(1024)S(1)}, u32[]{:S(2)}) copy-start(f32[1536]{0:T(1024)S(1)} %get-tuple-element.25) | copy-start | bytes 18436
  26.0 1.6 copy-start.32
  27.5 46.6 %copy-start.5 = (bf16[286,1536]{1,0:T(8,128)(2,1)}, bf16[286,1536]{1,0:T(8,128)(2,1)S(1)}, u32[]{:S(2)}) copy-start(bf16[286,1536]{1,0:T(8,128)(2,1)S(1)} %get-tuple-element.52) | copy-start | bytes 2635780
  74.1 2.4 copy-start.1
  90.2 1.1 copy-start.7
  90.2 2.8 copy-start.28
  91.3 1.7 copy-start.30
  94.1 1.2 copy-start.2
  95.3 5.6 %collective-permute-start.2 = (bf16[15,1536]{1,0:T(8,128)(2,1)S(1)}, bf16[15,1536]{1,0:T(8,128)(2,1)S(1)}, u32[]{:S(2)}, u32[]{:S(2)}) collective-permute-start(bf16[15,1536]{1,0:T(8,128)(2,1)S(1)} %get-tuple-element.50), channel_id=1, source_target_pairs={{0,8},{8,16},{16,24},{24,32},{32,40},{40,48},{48,56},{56,64},{64,7... | collective-permute-start | bytes 138248 | tf_op jit(solution)/shard_map/ppermute | solution.py:13
  99.5 6.0 %collective-permute-start.3 = (bf16[15,1536]{1,0:T(8,128)(2,1)S(1)}, bf16[15,1536]{1,0:T(8,128)(2,1)S(1)}, u32[]{:S(2)}, u32[]{:S(2)}) collective-permute-start(bf16[15,1536]{1,0:T(8,128)(2,1)S(1)} %get-tuple-element.49), channel_id=1, source_target_pairs={{8,0},{16,8},{24,16},{32,24},{40,32},{48,40},{56,48},{64,56},{72,6... | collective-permute-start | bytes 138248 | tf_op jit(solution)/shard_map/ppermute | solution.py:13
  106.2 10.6 %copy-start = (f32[286,1536]{1,0:T(8,128)S(1)}, f32[286,1536]{1,0:T(8,128)}, u32[]{:S(2)}) copy-start(f32[286,1536]{1,0:T(8,128)} %get-tuple-element.45) | copy-start | bytes 5271556
  116.8 2.3 copy-start.9
  116.9 3.2 copy-start.6
  119.1 0.9 copy-start.8
  125.2 0.9 copy-start.53
  125.2 2.1 copy-start.33
  125.2 2.2 copy-start.29
  125.3 2.2 copy-start.31
  125.3 4.2 %copy-start.3 = (f32[286,1536]{1,0:T(8,128)S(1)}, f32[286,1536]{1,0:T(8,128)}, u32[]{:S(2)}) copy-start(f32[286,1536]{1,0:T(8,128)} %get-tuple-element.51) | copy-start | bytes 5271556
  136.7 1.1 copy-start.4
  141.9 237.1 %collective-permute-start.4 = (bf16[128,1536]{1,0:T(8,128)(2,1)S(1)}, bf16[128,1536]{1,0:T(8,128)(2,1)S(1)}, u32[]{:S(2)}, u32[]{:S(2)}) collective-permute-start(bf16[128,1536]{1,0:T(8,128)(2,1)S(1)} %get-tuple-element.47), channel_id=1, source_target_pairs={{8,0},{16,8},{24,16},{32,24},{40,32},{48,40},{56,48},{64,56},{72,6... | collective-permute-start | bytes 1179656 | tf_op jit(solution)/shard_map/ppermute | solution.py:13
  143.2 235.8 %collective-permute-start.5 = (bf16[128,1536]{1,0:T(8,128)(2,1)S(1)}, bf16[128,1536]{1,0:T(8,128)(2,1)S(1)}, u32[]{:S(2)}, u32[]{:S(2)}) collective-permute-start(bf16[128,1536]{1,0:T(8,128)(2,1)S(1)} %get-tuple-element.48), channel_id=1, source_target_pairs={{0,8},{8,16},{16,24},{24,32},{32,40},{40,48},{48,56},{56,64},{64,7... | collective-permute-start | bytes 1179656 | tf_op jit(solution)/shard_map/ppermute | solution.py:13
  375.0 8.5 %collective-permute-start.6 = (bf16[8,3072]{1,0:T(8,128)(2,1)S(1)}, bf16[8,3072]{1,0:T(8,128)(2,1)S(1)}, u32[]{:S(2)}, u32[]{:S(2)}) collective-permute-start(bf16[8,3072]{1,0:T(8,128)(2,1)S(1)} %fusion), channel_id=1, source_target_pairs={{0,1},{1,2},{2,3},{3,4},{4,5},{5,6},{6,7},{8,9},{9,10},{10,11},{11... | collective-permute-start | bytes 147464
  376.9 6.6 %collective-permute-start.7 = (bf16[6,3072]{1,0:T(8,128)(2,1)S(1)}, bf16[6,3072]{1,0:T(8,128)(2,1)S(1)}, u32[]{:S(2)}, u32[]{:S(2)}) collective-permute-start(bf16[6,3072]{1,0:T(8,128)(2,1)S(1)} %slice.684), channel_id=1, source_target_pairs={{0,2},{1,3},{2,4},{3,5},{4,6},{5,7},{8,10},{9,11},{10,12},{11,13},... | collective-permute-start | bytes 110600
Sparse Core Ops, SparseCore 0:
  9.8 58.8 all-gather.1
  125.4 234.7 reduce-scatter.3
where the time goes:
time: 392 us; the launch traced here: 391 us
  waiting for transfers between devices  262 us (67%)
  other arithmetic  43.6 us (11%)
  starting transfers between devices  20 us (5%)
  between operations  18.5 us (5%)
  matrix products  16.6 us (4%)
  local copies, waits for them, and re-layouts  15.9 us (4%)
  blocking collectives  14.8 us (4%)
    reduce_scatter x1, waiting for transfers between devices, on_device(): lax.psum_scatter(rounded.astype(jnp.bfloat16), 'seq', scatter_dimension=0...  212 us
    all_gather x1, waiting for transfers between devices, on_device(): lax.all_gather(w_in, 'fsdp', axis=0, tiled=True)  41.1 us
    ppermute x6, starting transfers between devices, passed_along(): lax.ppermute(value, axis, [(source, source + steps) for source in range(i...  15.9 us
    unnamed x1, blocking collectives  14.8 us
    reduce_sum x2, other arithmetic, normalize_rows(): center = jnp.mean(values, axis=-1, keepdims=True)  14.2 us
    another operation x3, other arithmetic  13.7 us
  transfers between devices with their start and end apart: 10, of which 5 were waited for; matrix products, arithmetic and copies ran while one was open for 11% of the time, Pallas kernels for 0%

commit v1 on v0

--- a/solution.py
+++ b/solution.py
@@ -5,6 +5,27 @@
 from jax.sharding import PartitionSpec as P
 
 epsilon = 1e-05
+
+
+def collect(x, axis, dim):
+    size, here, span = (lax.axis_size(axis), lax.axis_index(axis), x.shape[dim])
+    right = [(i, (i + 1) % size) for i in range(size)]
+    left = [(i, (i - 1) % size) for i in range(size)]
+    result = jnp.zeros((*x.shape[:dim], size * span, *x.shape[dim + 1 :]), x.dtype)
+    result = lax.dynamic_update_slice_in_dim(result, x, here * span, axis=dim)
+    from_left = from_right = x
+    middle = size // 2
+    for step in range(1, middle + 1):
+        from_left = lax.ppermute(from_left, axis, right)
+        result = lax.dynamic_update_slice_in_dim(
+            result, from_left, (here - step) % size * span, axis=dim
+        )
+        if step < size - middle:
+            from_right = lax.ppermute(from_right, axis, left)
+            result = lax.dynamic_update_slice_in_dim(
+                result, from_right, (here + step) % size * span, axis=dim
+            )
+    return result
 
 
 def passed_along(value, axis, steps):
@@ -110,9 +131,7 @@
     labels = jnp.where(inside, labels, -1)
     normed, scale_inv = normalize_rows(rows_window)
     hidden = normed.astype(jnp.bfloat16)
-    projected = jnp.dot(
-        hidden, lax.all_gather(w_in, "fsdp", axis=0, tiled=True), preferred_element_type=jnp.float32
-    )
+    projected = jnp.dot(hidden, collect(w_in, "fsdp", 0), preferred_element_type=jnp.float32)
     values = projected[:, :model_width]
     gates = jax.nn.sigmoid(projected[:, model_width:])
     glu_out = (values * gates).astype(jnp.bfloat16)

time: 392 us -> 439 us (1.12)
  waiting for transfers between devices: 262 us -> 285 us
  local copies, waits for them, and re-layouts: 15.9 us -> 31.3 us
  starting transfers between devices: 20 us -> 26.9 us
    ppermute x0 -> x7, waiting for transfers between devices: none -> 64.2 us  [the longest x4 64.1 us: collect(): from_left = lax.ppermute(from_left, axis, right)]
    all_gather x1, waiting for transfers between devices: 41.1 us -> 0.01 us  [backward_product(): lax.all_gather(w_in, 'fsdp', axis=0, tiled=True)]
    dynamic_update_slice x0 -> x8, local copies, waits for them, and re-layouts: none -> 8.99 us  [the longest x4 4.51 us: collect(): lax.dynamic_update_slice_in_dim(result, from_left, (here - step) % size *...]
    ppermute x0 -> x7, starting transfers between devices: none -> 5.75 us  [the longest x3 5.7 us: collect(): from_right = lax.ppermute(from_right, axis, left)]
    broadcast_in_dim x0 -> x1, local copies, waits for them, and re-layouts: none -> 4.85 us  [collect(): jnp.zeros((*x.shape[:dim], size * span, *x.shape[dim + 1:]), x.dtype)]
  transfers between devices with their start and end apart: 10 -> 17, of which waited for: 5 -> 7; matrix products, arithmetic and copies ran while one was open for 11% -> 23% of each run, Pallas kernels for 0% -> 0%
where the time goes in v1:
time: 439 us; the launch traced here: 438 us
  waiting for transfers between devices  285 us (65%)
  other arithmetic  43.7 us (10%)
  local copies, waits for them, and re-layouts  31.3 us (7%)
  starting transfers between devices  26.9 us (6%)
  between operations  20.1 us (5%)
  matrix products  16.6 us (4%)
  blocking collectives  14.6 us (3%)
    reduce_scatter x1, waiting for transfers between devices, on_device(): lax.psum_scatter(rounded.astype(jnp.bfloat16), 'seq', scatter_dimension=0...  214 us
    ppermute x4, waiting for transfers between devices, collect(): from_left = lax.ppermute(from_left, axis, right)  64.1 us
    ppermute x6, starting transfers between devices, passed_along(): lax.ppermute(value, axis, [(source, source + steps) for source in range(i...  16.9 us
    reduce_sum x2, other arithmetic, normalize_rows(): center = jnp.mean(values, axis=-1, keepdims=True)  15.5 us
    unnamed x1, blocking collectives  14.6 us
    another operation x3, other arithmetic  13.7 us
  transfers between devices with their start and end apart: 17, of which 7 were waited for; matrix products, arithmetic and copies ran while one was open for 23% of the time, Pallas kernels for 0%

profile of v1, /device:TPU:8, one launch (start us, length us, event | category | flops | bytes accessed | tf_op | source)
XLA Modules:
  0.0 437.9 jit_solution(10614316564241914242)
XLA Ops:
  8.1 1.7 collective-permute-start.3
  9.8 4.6 %collective-permute-start = (bf16[128,1536]{1,0:T(8,128)(2,1)}, bf16[128,1536]{1,0:T(8,128)(2,1)}, u32[]{:S(2)}, u32[]{:S(2)}) collective-permute-start(bf16[128,1536]{1,0:T(8,128)(2,1)} %bitcast.21), channel_id=1, source_target_pairs={{0,8},{8,16},{16,24},{24,32},{32,40},{40,48},{48,56},{56,64},{64,7... | collective-permute-start | bytes 1179656 | tf_op jit(solution)/shard_map/ppermute | solution.py:34
  14.4 1.3 collective-permute-start.1
  15.7 1.4 constant_dynamic-slice_fusion.1
  17.8 0.8 reduce-window.4
  18.8 0.6 compare_convert_fusion.26
  19.4 2.6 slice_reduce_fusion.30
  22.0 0.7 compare_convert_fusion.29
  22.7 4.8 %broadcast_in_dim.44 = bf16[1536,3072]{1,0:T(8,128)(2,1)} broadcast(bf16[]{:T(256)} %constant.101.clone.1), dimensions={} | broadcast | bytes 9437186 | tf_op jit(solution)/shard_map/broadcast_in_dim | solution.py:14
  27.5 1.1 constant_dynamic-update-slice_fusion.7
  28.7 2.1 slice_reduce_fusion.29
  30.7 0.7 compare_convert_fusion.28
  31.4 0.7 pad_dynamic-slice_fusion.3
  33.5 0.6 iota_compare_fusion
  34.2 2.1 convert_reduce_fusion
  36.4 1.7 collective-permute-start.5
  38.0 0.4 fusion.3
  38.4 35.7 %collective-permute-done.4 = bf16[192,3072]{1,0:T(8,128)(2,1)S(1)} collective-permute-done((bf16[192,3072]{1,0:T(8,128)(2,1)S(1)}, bf16[192,3072]{1,0:T(8,128)(2,1)S(1)}, u32[]{:S(2)}, u32[]{:S(2)}) %collective-permute-start.4) | collective-permute-done | bytes 1179680 | tf_op jit(solution)/shard_map/ppermute | solution.py:19
  74.2 1.5 fusion.1
  75.7 1.2 constant_dynamic-update-slice_fusion.6
  77.0 2.3 collective-permute-start.7
  79.3 1.1 constant_dynamic-update-slice_fusion.5
  80.4 17.2 %collective-permute-done.6 = bf16[192,3072]{1,0:T(8,128)(2,1)S(1)} collective-permute-done((bf16[192,3072]{1,0:T(8,128)(2,1)S(1)}, bf16[192,3072]{1,0:T(8,128)(2,1)S(1)}, u32[]{:S(2)}, u32[]{:S(2)}) %collective-permute-start.6) | collective-permute-done | bytes 1179680 | tf_op jit(solution)/shard_map/ppermute | solution.py:19
  97.6 1.1 constant_dynamic-update-slice_fusion.4
  98.7 1.1 constant_dynamic-update-slice_fusion.3
  99.8 1.2 constant_dynamic-update-slice_fusion.2
  100.9 1.1 constant_dynamic-update-slice_fusion.1
  102.1 11.2 %collective-permute-done.8 = bf16[192,3072]{1,0:T(8,128)(2,1)S(1)} collective-permute-done((bf16[192,3072]{1,0:T(8,128)(2,1)S(1)}, bf16[192,3072]{1,0:T(8,128)(2,1)S(1)}, u32[]{:S(2)}, u32[]{:S(2)}) %collective-permute-start.8) | collective-permute-done | bytes 1179680 | tf_op jit(solution)/shard_map/ppermute | solution.py:19
  113.2 1.1 constant_dynamic-update-slice_fusion
  114.3 5.4 %fusion.90 = f32[286,3072]{1,0:T(8,128)S(1)} fusion(bf16[286,1536]{1,0:T(8,128)(2,1)S(1)} %get-tuple-element.52, bf16[1536,3072]{1,0:T(8,128)(2,1)} %constant_dynamic-update-slice_fusion), kind=kOutput, calls=%fused_computation.231 | convolution fusion | flops 2699034624 | bytes 13830144 | tf_op jit(solution)/shard_map/dot_general | solution.py:134
  120.2 2.0 fusion.6
  122.7 13.4 %fusion.86 = (f32[256]{0:T(256)S(1)}, f32[256,1536]{1,0:T(8,128)S(1)}) fusion(f32[256]{0:T(256)S(1)} %copy-done.45, bf16[286,1536]{1,0:T(8,128)(2,1)S(1)} %get-tuple-element.46, f32[1536]{0:T(1024)S(1)} %copy-done.39, f32[256]{0:T(256)S(1)} %copy-done.47, f32[1536]{0:T(1024)S(1)} %copy-done.40, f32[256]{0:T(256)S(1)} %copy-done.48, f32[1536]{0:T(1024)S(1)} %copy-done.11, ...), kind=kLoop, calls=%fused_computation.228 | loop fusion | flops 48365312 | bytes 26174464 | tf_op jit(solution)/shard_map/reduce_sum | solution.py:39
  136.1 0.3 multiply_reduce_fusion.2
  136.4 0.8 copy-done.8
  137.2 1.1 fusion.84
  138.3 0.5 multiply_select_fusion
  138.8 1.1 copy-done.2
  140.0 3.7 collective-permute-start.9
  143.7 0.6 pad.4.clone
  144.4 1.5 collective-permute-start.10
  145.9 1.6 maximum_maximum_fusion
  147.5 2.9 collective-permute-done.10
  150.4 0.8 add.396
  151.2 10.6 %multiply_convert_fusion.1 = (bf16[256,1536]{1,0:T(8,128)(2,1)S(1)}, f32[256,1536]{1,0:T(8,128)S(1)}) fusion(f32[286,1536]{1,0:T(8,128)} %get-tuple-element.45, f32[256]{0:T(256)} %get-tuple-element.53, f32[286,1536]{1,0:T(8,128)S(1)} %add.396, f32[1536]{0:T(1024)} %get-tuple-element.36, f32[256]{0:T(256)} %get-tuple-element.62, ...), kind=kLoop, calls=%fused_computation.115 | loop fusion | flops 36962304 | bytes 52912384 | tf_op jit(solution)/shard_map/convert
  161.8 2.3 fusion.10
  164.1 0.9 copy-done.9
  165.0 5.2 %convolution_convert_fusion = bf16[1536,3072]{1,0:T(8,128)(2,1)} fusion(bf16[256,1536]{1,0:T(8,128)(2,1)S(1)} %fusion.10, bf16[256,1536]{1,0:T(8,128)(2,1)S(1)} %get-tuple-element.38, bf16[286,1536]{1,0:T(8,128)(2,1)S(1)} %copy-done.7), kind=kOutput, calls=%fused_computation | convolution fusion | flops 2423783424 | bytes 11796480 | tf_op jit(solution)/shard_map/dot_general | solution.py:87
  171.0 0.6 dynamic-slice.8
  172.4 1.5 select_bitcast_fusion
  173.8 5.9 %fusion.83 = (f32[256]{0:T(256)S(1)}, f32[256]{0:T(256)S(1)}, f32[256,1536]{1,0:T(8,128)S(1)}) fusion(f32[286,1536]{1,0:T(8,128)S(1)} %copy-done.3, bf16[1536,3072]{1,0:T(8,128)(2,1)} %all-gather.2.cloned.1.call-done, bf16[256,1536]{1,0:T(8,128)(2,1)} %copy-done.9, bf16[256,1536]{1,0:T(8,128)(2,1)} %copy-done.10), kind=kOutput, calls=%fused_computation.226 | convolution fusion | flops 2420243968 | bytes 14157824 | tf_op jit(solution)/shard_map/dot_general | solution.py:114
  179.8 1.3 multiply_convert_fusion
  181.1 0.1 broadcast_in_dim.48
  181.2 1.0 copy-done.5
  182.2 4.0 dynamic_update_slice.39
  186.3 1.3 collective-permute-start.11
  187.6 4.6 %collective-permute-start.12 = (bf16[128,1536]{1,0:T(8,128)(2,1)S(1)}, bf16[128,1536]{1,0:T(8,128)(2,1)S(1)}, u32[]{:S(2)}, u32[]{:S(2)}) collective-permute-start(bf16[128,1536]{1,0:T(8,128)(2,1)S(1)} %get-tuple-element.48), channel_id=1, source_target_pairs={{0,8},{8,16},{16,24},{24,32},{32,40},{40,48},{48,56},{56,64},{64,7... | collective-permute-start | bytes 1179656 | tf_op jit(solution)/shard_map/ppermute | solution.py:34
  192.1 214.1 %reduce-scatter.4.cloned.1.call-done = bf16[48,3072]{1,0:T(8,128)(2,1)} async-done(((bf16[1536,3072]{1,0:T(8,128)(2,1)}), bf16[48,3072]{1,0:T(8,128)(2,1)}) %reduce-scatter.4.cloned.1.call-update) | async-done | bytes 294928 | tf_op jit(solution)/shard_map/reduce_scatter | solution.py:178
  406.2 14.6 %fusion = bf16[8,3072]{1,0:T(8,128)(2,1)S(1)} fusion(bf16[48,3072]{1,0:T(8,128)(2,1)} %reduce-scatter.4.cloned.1.call-done), kind=kCustom, calls=%all-reduce-scatter | all-reduce-scatter fusion | flops 196609 | bytes 345088
  420.9 1.9 collective-permute-start.13
  422.8 2.3 collective-permute-start.14
  425.1 0.9 fusion.79
  426.0 3.4 collective-permute-done.14
  429.4 0.3 concatenate.16
  429.7 0.7 convert_multiply_fusion
  (167 shorter events, 1.0 us)
Async XLA Ops:
  8.0 165.8 %all-gather.2.cloned.1.call-start = ((), (), s32[]{:S(2)}) async-start(), calls=%async_computation.1 | async-start | bytes 10616832 | tf_op jit(solution)/shard_map/all_gather | solution.py:116
  8.0 25.4 %collective-permute-start.2 = (bf16[192,3072]{1,0:T(8,128)(2,1)}, bf16[192,3072]{1,0:T(8,128)(2,1)S(1)}, u32[]{:S(2)}, u32[]{:S(2)}) collective-permute-start(bf16[192,3072]{1,0:T(8,128)(2,1)} %param.9), channel_id=1, source_target_pairs={{0,1},{1,2},{2,3},{3,4},{4,5},{5,6},{6,7},{7,0},{8,9},{9,10},{10,1... | collective-permute-start | bytes 3538952 | tf_op jit(solution)/shard_map/ppermute | solution.py:19
  8.1 28.3 %collective-permute-start.3 = (bf16[192,3072]{1,0:T(8,128)(2,1)}, bf16[192,3072]{1,0:T(8,128)(2,1)S(1)}, u32[]{:S(2)}, u32[]{:S(2)}) collective-permute-start(bf16[192,3072]{1,0:T(8,128)(2,1)} %param.9), channel_id=1, source_target_pairs={{0,7},{1,0},{2,1},{3,2},{4,3},{5,4},{6,5},{7,6},{8,15},{9,8},{10,9... | collective-permute-start | bytes 3538952 | tf_op jit(solution)/shard_map/ppermute | solution.py:24
  9.8 24.4 %collective-permute-start = (bf16[128,1536]{1,0:T(8,128)(2,1)}, bf16[128,1536]{1,0:T(8,128)(2,1)}, u32[]{:S(2)}, u32[]{:S(2)}) collective-permute-start(bf16[128,1536]{1,0:T(8,128)(2,1)} %bitcast.21), channel_id=1, source_target_pairs={{0,8},{8,16},{16,24},{24,32},{32,40},{40,48},{48,56},{56,64},{64,7... | collective-permute-start | bytes 1179656 | tf_op jit(solution)/shard_map/ppermute | solution.py:34
  14.4 19.9 %collective-permute-start.1 = (bf16[128,1536]{1,0:T(8,128)(2,1)}, bf16[128,1536]{1,0:T(8,128)(2,1)}, u32[]{:S(2)}, u32[]{:S(2)}) collective-permute-start(bf16[128,1536]{1,0:T(8,128)(2,1)} %bitcast.22), channel_id=1, source_target_pairs={{8,0},{16,8},{24,16},{32,24},{40,32},{48,40},{56,48},{64,56},{72,6... | collective-permute-start | bytes 1179656 | tf_op jit(solution)/shard_map/ppermute | solution.py:34
  15.7 390.6 %reduce-scatter.4.cloned.1.call-start = ((), (), s32[]{:S(2)}) async-start(), calls=%async_computation.2 | async-start | bytes 9732096 | tf_op jit(solution)/shard_map/reduce_scatter | solution.py:178
  19.4 102.8 %copy-start.43 = (f32[256]{0:T(256)}, f32[256]{0:T(256)S(1)}, u32[]{:S(2)}) copy-start(f32[256]{0:T(256)S(1)} %get-tuple-element.80) | copy-start | bytes 3076
  22.7 4.9 %copy-start.4 = (bf16[192,3072]{1,0:T(8,128)(2,1)S(1)}, bf16[192,3072]{1,0:T(8,128)(2,1)}, u32[]{:S(2)}) copy-start(bf16[192,3072]{1,0:T(8,128)(2,1)} %param.9) | copy-start | bytes 3538948
  33.4 40.7 %collective-permute-start.4 = (bf16[192,3072]{1,0:T(8,128)(2,1)S(1)}, bf16[192,3072]{1,0:T(8,128)(2,1)S(1)}, u32[]{:S(2)}, u32[]{:S(2)}) collective-permute-start(bf16[192,3072]{1,0:T(8,128)(2,1)S(1)} %collective-permute-done.2), channel_id=1, source_target_pairs={{0,1},{1,2},{2,3},{3,4},{4,5},{5,6},{6,7},{7,0},{8,9},{9,10},{10,1... | collective-permute-start | bytes 3538952 | tf_op jit(solution)/shard_map/ppermute | solution.py:19
  34.1 88.1 %copy-start.54 = (f32[256]{0:T(256)}, f32[256]{0:T(256)S(1)}, u32[]{:S(2)}) copy-start(f32[256]{0:T(256)S(1)} %get-tuple-element.71) | copy-start | bytes 3076
  34.1 88.1 %copy-start.55 = (f32[256]{0:T(256)}, f32[256]{0:T(256)S(1)}, u32[]{:S(2)}) copy-start(f32[256]{0:T(256)S(1)} %get-tuple-element.72) | copy-start | bytes 3076
  34.1 88.1 %copy-start.56 = (f32[256]{0:T(256)}, f32[256]{0:T(256)S(1)}, u32[]{:S(2)}) copy-start(f32[256]{0:T(256)S(1)} %get-tuple-element.73) | copy-start | bytes 3076
  34.2 88.1 %copy-start.57 = (f32[256]{0:T(256)}, f32[256]{0:T(256)S(1)}, u32[]{:S(2)}) copy-start(f32[256]{0:T(256)S(1)} %get-tuple-element.74) | copy-start | bytes 3076
  34.2 88.1 %copy-start.58 = (f32[256]{0:T(256)}, f32[256]{0:T(256)S(1)}, u32[]{:S(2)}) copy-start(f32[256]{0:T(256)S(1)} %get-tuple-element.75) | copy-start | bytes 3076
  34.2 88.1 %copy-start.59 = (f32[256]{0:T(256)}, f32[256]{0:T(256)S(1)}, u32[]{:S(2)}) copy-start(f32[256]{0:T(256)S(1)} %get-tuple-element.76) | copy-start | bytes 3076
  34.2 88.1 %copy-start.60 = (f32[256]{0:T(256)}, f32[256]{0:T(256)S(1)}, u32[]{:S(2)}) copy-start(f32[256]{0:T(256)S(1)} %get-tuple-element.77) | copy-start | bytes 3076
  34.2 88.1 %copy-start.61 = (f32[256]{0:T(256)}, f32[256]{0:T(256)S(1)}, u32[]{:S(2)}) copy-start(f32[256]{0:T(256)S(1)} %get-tuple-element.78) | copy-start | bytes 3076
  34.2 88.1 %copy-start.62 = (f32[256]{0:T(256)}, f32[256]{0:T(256)S(1)}, u32[]{:S(2)}) copy-start(f32[256]{0:T(256)S(1)} %get-tuple-element.79) | copy-start | bytes 3076
  36.4 40.6 %collective-permute-start.5 = (bf16[192,3072]{1,0:T(8,128)(2,1)S(1)}, bf16[192,3072]{1,0:T(8,128)(2,1)S(1)}, u32[]{:S(2)}, u32[]{:S(2)}) collective-permute-start(bf16[192,3072]{1,0:T(8,128)(2,1)S(1)} %collective-permute-done.3), channel_id=1, source_target_pairs={{0,7},{1,0},{2,1},{3,2},{4,3},{5,4},{6,5},{7,6},{8,15},{9,8},{10,9... | collective-permute-start | bytes 3538952 | tf_op jit(solution)/shard_map/ppermute | solution.py:24
  38.4 37.3 %copy-start.41 = (f32[286]{0:T(512)}, f32[286]{0:T(512)S(1)}, u32[]{:S(2)}) copy-start(f32[286]{0:T(512)S(1)} %add_rsqrt_fusion) | copy-start | bytes 3436
  74.2 23.4 %collective-permute-start.6 = (bf16[192,3072]{1,0:T(8,128)(2,1)S(1)}, bf16[192,3072]{1,0:T(8,128)(2,1)S(1)}, u32[]{:S(2)}, u32[]{:S(2)}) collective-permute-start(bf16[192,3072]{1,0:T(8,128)(2,1)S(1)} %collective-permute-done.4), channel_id=1, source_target_pairs={{0,1},{1,2},{2,3},{3,4},{4,5},{5,6},{6,7},{7,0},{8,9},{9,10},{10,1... | collective-permute-start | bytes 3538952 | tf_op jit(solution)/shard_map/ppermute | solution.py:19
  75.7 38.6 %copy-start.6 = (bf16[286,1536]{1,0:T(8,128)(2,1)}, bf16[286,1536]{1,0:T(8,128)(2,1)S(1)}, u32[]{:S(2)}) copy-start(bf16[286,1536]{1,0:T(8,128)(2,1)S(1)} %get-tuple-element.52) | copy-start | bytes 2635780
  77.0 23.9 %collective-permute-start.7 = (bf16[192,3072]{1,0:T(8,128)(2,1)S(1)}, bf16[192,3072]{1,0:T(8,128)(2,1)S(1)}, u32[]{:S(2)}, u32[]{:S(2)}) collective-permute-start(bf16[192,3072]{1,0:T(8,128)(2,1)S(1)} %collective-permute-done.5), channel_id=1, source_target_pairs={{0,7},{1,0},{2,1},{3,2},{4,3},{5,4},{6,5},{7,6},{8,15},{9,8},{10,9... | collective-permute-start | bytes 3538952 | tf_op jit(solution)/shard_map/ppermute | solution.py:24
  97.6 15.6 %collective-permute-start.8 = (bf16[192,3072]{1,0:T(8,128)(2,1)S(1)}, bf16[192,3072]{1,0:T(8,128)(2,1)S(1)}, u32[]{:S(2)}, u32[]{:S(2)}) collective-permute-start(bf16[192,3072]{1,0:T(8,128)(2,1)S(1)} %collective-permute-done.6), channel_id=1, source_target_pairs={{0,1},{1,2},{2,3},{3,4},{4,5},{5,6},{6,7},{7,0},{8,9},{9,10},{10,1... | collective-permute-start | bytes 3538952 | tf_op jit(solution)/shard_map/ppermute | solution.py:19
  119.8 2.5 copy-start.11
  119.8 2.5 copy-start.12
  119.8 2.5 copy-start.13
  119.8 2.5 copy-start.14
  119.8 2.5 copy-start.15
  119.9 2.5 copy-start.16
  119.9 2.5 copy-start.17
  119.9 2.5 copy-start.18
  119.9 2.5 copy-start.19
  119.9 2.5 copy-start.20
  119.9 2.5 copy-start.21
  119.9 2.5 copy-start.22
  119.9 2.5 copy-start.23
  119.9 2.5 copy-start.24
  119.9 2.5 copy-start.25
  120.0 2.5 copy-start.26
  120.0 2.5 copy-start.27
  120.0 2.5 copy-start.28
  120.0 2.5 copy-start.29
  120.0 2.5 copy-start.30
  120.0 2.5 copy-start.31
  120.0 2.5 copy-start.32
  120.0 2.5 copy-start.33
  120.0 2.5 copy-start.34
  120.1 2.5 copy-start.35
  120.1 2.5 copy-start.36
  120.1 2.5 copy-start.37
  120.1 2.5 copy-start.38
  120.1 2.5 copy-start.39
  120.1 2.5 copy-start.40
  120.1 2.5 copy-start.44
  140.0 5.8 %collective-permute-start.9 = (bf16[15,1536]{1,0:T(8,128)(2,1)S(1)}, bf16[15,1536]{1,0:T(8,128)(2,1)S(1)}, u32[]{:S(2)}, u32[]{:S(2)}) collective-permute-start(bf16[15,1536]{1,0:T(8,128)(2,1)S(1)} %get-tuple-element.50), channel_id=1, source_target_pairs={{0,8},{8,16},{16,24},{24,32},{32,40},{40,48},{48,56},{56,64},{64,7... | collective-permute-start | bytes 138248 | tf_op jit(solution)/shard_map/ppermute | solution.py:34
  144.4 6.0 %collective-permute-start.10 = (bf16[15,1536]{1,0:T(8,128)(2,1)S(1)}, bf16[15,1536]{1,0:T(8,128)(2,1)S(1)}, u32[]{:S(2)}, u32[]{:S(2)}) collective-permute-start(bf16[15,1536]{1,0:T(8,128)(2,1)S(1)} %get-tuple-element.49), channel_id=1, source_target_pairs={{8,0},{16,8},{24,16},{32,24},{40,32},{48,40},{56,48},{64,56},{72,6... | collective-permute-start | bytes 138248 | tf_op jit(solution)/shard_map/ppermute | solution.py:34
  151.2 10.6 %copy-start = (f32[286,1536]{1,0:T(8,128)S(1)}, f32[286,1536]{1,0:T(8,128)}, u32[]{:S(2)}) copy-start(f32[286,1536]{1,0:T(8,128)} %get-tuple-element.45) | copy-start | bytes 5271556
  161.8 3.2 copy-start.7
  170.2 3.6 copy-start.3
  186.3 238.8 %collective-permute-start.11 = (bf16[128,1536]{1,0:T(8,128)(2,1)S(1)}, bf16[128,1536]{1,0:T(8,128)(2,1)S(1)}, u32[]{:S(2)}, u32[]{:S(2)}) collective-permute-start(bf16[128,1536]{1,0:T(8,128)(2,1)S(1)} %get-tuple-element.47), channel_id=1, source_target_pairs={{8,0},{16,8},{24,16},{32,24},{40,32},{48,40},{56,48},{64,56},{72,6... | collective-permute-start | bytes 1179656 | tf_op jit(solution)/shard_map/ppermute | solution.py:34
  187.6 237.5 %collective-permute-start.12 = (bf16[128,1536]{1,0:T(8,128)(2,1)S(1)}, bf16[128,1536]{1,0:T(8,128)(2,1)S(1)}, u32[]{:S(2)}, u32[]{:S(2)}) collective-permute-start(bf16[128,1536]{1,0:T(8,128)(2,1)S(1)} %get-tuple-element.48), channel_id=1, source_target_pairs={{0,8},{8,16},{16,24},{24,32},{32,40},{40,48},{48,56},{56,64},{64,7... | collective-permute-start | bytes 1179656 | tf_op jit(solution)/shard_map/ppermute | solution.py:34
  420.9 8.5 %collective-permute-start.13 = (bf16[8,3072]{1,0:T(8,128)(2,1)S(1)}, bf16[8,3072]{1,0:T(8,128)(2,1)S(1)}, u32[]{:S(2)}, u32[]{:S(2)}) collective-permute-start(bf16[8,3072]{1,0:T(8,128)(2,1)S(1)} %fusion), channel_id=1, source_target_pairs={{0,1},{1,2},{2,3},{3,4},{4,5},{5,6},{6,7},{8,9},{9,10},{10,11},{11... | collective-permute-start | bytes 147464
  422.8 6.6 %collective-permute-start.14 = (bf16[6,3072]{1,0:T(8,128)(2,1)S(1)}, bf16[6,3072]{1,0:T(8,128)(2,1)S(1)}, u32[]{:S(2)}, u32[]{:S(2)}) collective-permute-start(bf16[6,3072]{1,0:T(8,128)(2,1)S(1)} %slice.684), channel_id=1, source_target_pairs={{0,2},{1,3},{2,4},{3,5},{4,6},{5,7},{8,10},{9,11},{10,12},{11,13},... | collective-permute-start | bytes 110600
  (19 other events, 37.6 us)
Sparse Core Ops, SparseCore 0:
  15.8 75.3 all-gather.1
Sparse Core Ops, SparseCore 1:
  170.3 235.9 reduce-scatter.3
